TPU v7x, 32 devices: a whole 2x2x4 slice. The times are simulated.
32 devices in a mesh: leaf: 8 (over z, y), rhs: 4 (over x, core).
Axes of the slice: x: 2, y: 2, z: 4, core: 2. Of those that a mesh axis runs over, the one named last changes fastest.
Arguments:
- obs_coef: float32 [128, 2048], P('rhs', 'leaf'), may hold values from -0.75 to 0.75
- obs_data: float32 [320, 2048], P('rhs', 'leaf'), may hold values from -6 to 6
- obs_target: int32 [2048], P('leaf'), may hold values from 0 to 31, as said below
- leaf_map: int32 [32], replicated, may hold values from 0 to 31, as said below
- leaf_parent: int32 [32], replicated, may hold values from 0 to 7
- leaf_inv: float32 [32, 128, 128], P('leaf'), may hold values from -0.5 to 1.5
- leaf_off: float32 [32, 128, 128], P('leaf'), may hold values from -0.25 to 0.25
- top_inv: float32 [8, 128, 128], replicated, may hold values from -0.5 to 1.5
- top_rhs: float32 [8, 320, 128], P(None, 'rhs'), may hold values from -6 to 6
Outputs:
- leaf_solution: float32 [32, 320, 128], P('leaf', 'rhs')
- top_solution: float32 [8, 320, 128], P(None, 'rhs')
Inputs may be any that keep to these rules, and one draw needn't show every extreme that they name: A permutation: supernode i is stored at position leaf_map[i], which lies on index leaf_map[i] // 4 of leaf. `obs_target`: the rows held by one index of leaf name supernodes stored on any one index of leaf at most 64 times; in every draw one index of leaf is named exactly 64 times by the rows of every index.
All inputs are finite; a program needn't handle non-finite values.
Results may differ from a plain program's by a relative error of at most 0.0003.
Values sent between devices are 32-bit elements; how exact they have to be, the bound alone decides.
A program may use at most 64 MiB of HBM per device.

v0:
```python
import functools

import jax
import jax.numpy as jnp
from jax import lax
from jax.experimental import pallas as pl
from jax.experimental.pallas import tpu as pltpu
from jax.sharding import PartitionSpec as P

F32, BF16 = jnp.float32, jnp.bfloat16
MESH = pl.DeviceIdType.MESH
LANES = 128


def split(x):
    high = x.astype(BF16)
    return high, (x - high.astype(F32)).astype(BF16)


def contract(a, b, ca, cb):
    return lax.dot_general(a, b, (((ca,), (cb,)), ((), ())), preferred_element_type=F32)


def dot3(a, b, ca, cb):
    (ah, al), (bh, bl) = a, b
    return contract(ah, bh, ca, cb) + (contract(ah, bl, ca, cb) + contract(al, bh, ca, cb))


def flipped(index, bits, count):
    out = index
    place = 1
    while place < count:
        if bits & place:
            out = out + place * (1 - 2 * lax.rem(lax.div(index, place), 2))
        place *= 2
    return out


def kernel(
    groups, shards, capacity,
    tgt_h, coef_h, data_h, lmap_h, lpar_h, inv_h, off_h, tinv_h, trhs_h,
    leaf_out, top_out,
    tgt, coef, data, lmap, lpar, inv, off, tinv, trhs,
    send, recv, packed, wide, base, parts, across, joined, along,
    d_send, d_recv, f_send, f_recv, a_send, a_recv, z_send, z_recv, g_send, g_recv, l_sem,
):
    me = lax.axis_index("leaf")
    shard = lax.axis_index("rhs")
    local, width = inv.shape[0], inv.shape[1]
    coef_rows, rows = coef.shape
    dates = data.shape[0]
    top_each = tinv.shape[0]
    total = lmap.shape[0]
    fold = LANES // coef_rows
    piece = capacity // fold
    pair = f_send.shape[1]
    cuts, tops_all, half = parts.shape[0], parts.shape[1], parts.shape[2]
    per = groups // pair
    leaf_peers = [flipped(me, o, groups) for o in range(groups)]
    far_first = sorted(range(1, groups), key=lambda o: (-(o.bit_length()), o))
    order = [0]
    for o in range(groups // 2):
        order += [groups // 2 + o] + ([o + 1] if o + 1 < groups // 2 else [])
    rhs_peers = [lax.rem(shard + o, shards) for o in range(shards)]

    barrier = pltpu.get_barrier_semaphore()
    for o in range(1, groups):
        pl.semaphore_signal(barrier, inc=1, device_id=(leaf_peers[o], shard), device_id_type=MESH)
    for o in range(1, shards):
        pl.semaphore_signal(barrier, inc=1, device_id=(me, rhs_peers[o]), device_id_type=MESH)
    tops = pl.ds(me * top_each, top_each)
    loads = []
    for i, (src, dst) in enumerate(
        [
            (tgt_h, tgt),
            (lmap_h, lmap),
            (coef_h, coef),
            (data_h, data),
            (lpar_h, lpar),
            (inv_h, inv),
            (off_h, off),
            (tinv_h.at[tops], tinv),
            (trhs_h.at[tops], trhs),
        ]
    ):
        copy = pltpu.make_async_copy(src, dst, l_sem.at[i])
        copy.start()
        loads.append(copy)
    loads[0].wait()
    loads[1].wait()

    target = tgt[...]
    position = jnp.zeros_like(target)
    for i in range(total):
        position = jnp.where(target == i, lmap[i], position)
    place = lax.broadcasted_iota(jnp.int32, (groups, rows), 0)
    first = jnp.zeros_like(place)
    for o in range(groups):
        first = jnp.where(place == o, leaf_peers[o] * local, first)
    member = jnp.broadcast_to(position, (groups, rows)) - first
    owned = (member >= 0) & (member < local)
    hot = jnp.where(owned, 1.0, 0.0)
    before = (
        lax.broadcasted_iota(jnp.int32, (rows, rows), 0)
        < lax.broadcasted_iota(jnp.int32, (rows, rows), 1)
    )
    rank = contract(hot.astype(BF16), jnp.where(before, 1.0, 0.0).astype(BF16), 1, 0)
    slot = jnp.where(owned, rank.astype(jnp.int32), -1)
    mark = jnp.sum(hot * (member + 1).astype(F32), axis=0, keepdims=True)
    slot_ids = lax.broadcasted_iota(jnp.int32, (capacity, rows), 0)
    loads[2].wait()
    loads[3].wait()
    gap = lambda n: [jnp.zeros((n, rows), F32)] if n else []
    coef_fields = split(
        jnp.concatenate(
            [
                jnp.concatenate(
                    gap(q * coef_rows) + [coef[...]] + gap((fold - 1 - q) * coef_rows), axis=0
                )
                for q in range(fold)
            ],
            axis=1,
        )
    )
    marks = jnp.broadcast_to(mark, (8, rows))
    date_fields = split(
        jnp.concatenate(
            [
                jnp.concatenate([data[: dates // 2], marks], axis=0),
                jnp.concatenate([data[dates // 2 :], marks], axis=0),
            ],
            axis=1,
        )
    )

    def place_rows(o, i):
        chosen = jnp.where(slot_ids == slot[o : o + 1, :], 1.0, 0.0)
        folded = jnp.concatenate(
            [chosen[q * piece : (q + 1) * piece] for q in range(fold)], axis=1
        ).astype(BF16)
        none = jnp.zeros_like(chosen)
        doubled = jnp.concatenate(
            [
                jnp.concatenate([chosen, none], axis=1),
                jnp.concatenate([none, chosen], axis=1),
            ],
            axis=0,
        ).astype(BF16)
        send[i, :piece] = contract(folded, coef_fields[0], 1, 1) + contract(
            folded, coef_fields[1], 1, 1
        )
        send[i, piece:] = contract(date_fields[0], doubled, 1, 1) + contract(
            date_fields[1], doubled, 1, 1
        )

    pl.semaphore_wait(barrier, groups - 1 + shards - 1)
    row_copies = {}
    for i in range(1, groups):
        o = order[i]
        place_rows(o, i)
        copy = pltpu.make_async_remote_copy(
            src_ref=send.at[i],
            dst_ref=recv.at[i],
            send_sem=d_send.at[i],
            recv_sem=d_recv.at[i],
            device_id=(leaf_peers[o], shard),
            device_id_type=MESH,
        )
        copy.start()
        row_copies[i] = copy
    place_rows(0, 0)
    recv[0] = send[0]

    for copy in loads[4:]:
        copy.wait()
    for l in range(local):
        high, low = split(dot3(split(off[l]), split(inv[l]), 1, 0))
        wide[0, l] = high
        wide[1, l] = low
    gram = []
    for i in range(top_each):
        block = split(tinv[i])
        gram.append(split(dot3(block, block, 0, 0)))
    up = []
    for l in range(local):
        found = jnp.int32(0)
        for i in range(total):
            found = jnp.where(lmap[i] == me * local + l, lpar[i], found)
        up.append(found)

    forwards = []
    for g in range(pair):
        for i in range(g * per, (g + 1) * per):
            if i > 0:
                row_copies[i].wait_recv()
            packed[shard, i] = recv[i, :piece]
        span = pl.ds(g * per, per)
        for o in range(1, shards):
            copy = pltpu.make_async_remote_copy(
                src_ref=recv.at[span, pl.ds(0, piece)],
                dst_ref=packed.at[shard, span],
                send_sem=f_send.at[o, g],
                recv_sem=f_recv.at[o, g],
                device_id=(me, rhs_peers[o]),
                device_id_type=MESH,
            )
            copy.start()
            forwards.append(copy)
    ready = len(forwards) // 2
    span = groups // 2
    big_group = lax.broadcasted_iota(jnp.int32, (span * piece, LANES), 1) // coef_rows
    rhs_all = None
    first_half = lax.broadcasted_iota(jnp.int32, (recv.shape[1] - piece, LANES), 1) < capacity
    for part in range(2):
        here = slice(part * span, (part + 1) * span)
        series, marked = [], []
        for i in range(part * span, (part + 1) * span, 2):
            one, two = recv[i, piece:], recv[i + 1, piece:]
            early = jnp.where(first_half, one, pltpu.roll(two, capacity, 1))
            late = jnp.where(first_half, pltpu.roll(one, capacity, 1), two)
            series.append(jnp.concatenate([early[: dates // 2], late[: dates // 2]], axis=0))
            marked.append(early[dates // 2 : dates // 2 + 1])
        series = jnp.concatenate(series, axis=1)
        marked = jnp.concatenate(marked, axis=1)
        spread = split(
            jnp.concatenate(
                [jnp.where(marked == float(l + 1), series, 0.0) for l in range(local)], axis=0
            )
        )
        for copy in forwards[part * ready : (part + 1) * ready]:
            copy.wait_recv()
        packs = [packed[s, here].reshape(span * piece, LANES) for s in range(shards)]
        pieces = []
        for q in range(fold):
            out = None
            for s in range(shards):
                shift = ((s - q) * coef_rows) % LANES
                moved = pltpu.roll(packs[s], shift, 1) if shift else packs[s]
                out = moved if out is None else jnp.where(big_group == s, moved, out)
            pieces.append(out.reshape(span, 1, piece, LANES))
        coefs = jnp.concatenate(pieces, axis=1).reshape(span * capacity, LANES)
        term = dot3(spread, split(coefs), 1, 0)
        rhs_all = term if rhs_all is None else rhs_all + term
    rhs = [
        [split(rhs_all[l * dates + n : l * dates + n + half]) for l in range(local)]
        for n in range(0, dates, half)
    ]
    steps = [h // 2 for h in far_first if h % 2 == 0] + [0]
    cross, sums, solutions = {}, {}, {}
    weight = [[jnp.where(up[l] == p, 1.0, 0.0) for p in range(tops_all)] for l in range(local)]
    for n in range(cuts):
        updates = [dot3(rhs[n][l], (wide[0, l], wide[1, l]), 1, 1) for l in range(local)]
        for p in range(tops_all):
            acc = weight[0][p] * updates[0]
            for l in range(1, local):
                acc = acc + weight[l][p] * updates[l]
            parts[n, p] = acc
        for h in steps:
            copy = pltpu.make_async_remote_copy(
                src_ref=parts.at[n, pl.ds(leaf_peers[2 * h + 1] * top_each, top_each)],
                dst_ref=across.at[n, h],
                send_sem=a_send.at[n, h],
                recv_sem=a_recv.at[n, h],
                device_id=(leaf_peers[1], shard),
                device_id_type=MESH,
            )
            copy.start()
            cross[n, h] = copy
    residue = []
    for n in range(cuts):
        for h in steps:
            cross[n, h].wait_recv()
            here = parts[n, pl.ds(leaf_peers[2 * h] * top_each, top_each)] + across[n, h]
            if h == 0:
                residue.append(trhs[:, n * half : (n + 1) * half] - here)
                continue
            joined[n, h] = here
            copy = pltpu.make_async_remote_copy(
                src_ref=joined.at[n, h],
                dst_ref=along.at[n, h],
                send_sem=z_send.at[n, h],
                recv_sem=z_recv.at[n, h],
                device_id=(leaf_peers[2 * h], shard),
                device_id_type=MESH,
            )
            copy.start()
            sums[n, h] = copy
    for l in range(local):
        factor = split(inv[l])
        for n in range(cuts):
            solved = split(dot3(rhs[n][l], factor, 1, 1))
            base[l, n * half : (n + 1) * half] = dot3(solved, factor, 1, 0)

    def pass_on(n, h, o, peer):
        block = top_out.at[pl.ds(leaf_peers[h] * top_each, top_each), pl.ds(n * half, half)]
        copy = pltpu.make_async_remote_copy(
            src_ref=block,
            dst_ref=block,
            send_sem=g_send.at[n, o],
            recv_sem=g_recv.at[n, o],
            device_id=(leaf_peers[peer], shard),
            device_id_type=MESH,
        )
        copy.start()
        solutions[n, o] = copy

    for n in range(cuts):
        left = residue[n]
        for h in steps[:-1]:
            sums[n, h].wait_recv()
            left = left - along[n, h]
        for i in range(top_each):
            top_out[me * top_each + i, n * half : (n + 1) * half] = dot3(
                split(left[i]), gram[i], 1, 0
            )
        for h in steps[:-1]:
            pass_on(n, 0, 2 * h, 2 * h)
        pass_on(n, 0, 1, 1)
    for n in range(cuts):
        for h in reversed(steps[:-1]):
            solutions[n, 2 * h].wait_recv()
            pass_on(n, 2 * h, 2 * h + 1, 1)
    for copy in [*row_copies.values(), *forwards, *cross.values(), *sums.values()]:
        copy.wait_send()
    for n in range(cuts):
        for h in reversed(steps):
            solutions[n, 2 * h + 1].wait_recv()
        dates_here = slice(n * half, (n + 1) * half)
        for l in range(local):
            own = weight[l][0] * top_out[0, dates_here]
            for p in range(1, tops_all):
                own = own + weight[l][p] * top_out[p, dates_here]
            lifted = dot3(split(own), (wide[0, l], wide[1, l]), 1, 0)
            leaf_out[l, dates_here] = base[l, dates_here] - lifted
    for copy in solutions.values():
        copy.wait_send()


def write_out(leaf_v, top_v, leaf_h, top_h, sems):
    copies = [
        pltpu.make_async_copy(leaf_v, leaf_h, sems.at[0]),
        pltpu.make_async_copy(top_v, top_h, sems.at[1]),
    ]
    for copy in copies:
        copy.start()
    for copy in copies:
        copy.wait()


def fused(
    obs_coef, obs_data, obs_target, leaf_map, leaf_parent, leaf_inv, leaf_off, top_inv, top_rhs
):
    groups, shards = lax.axis_size("leaf"), lax.axis_size("rhs")
    rows = obs_target.shape[0]
    capacity = 2 * rows // groups
    local, width = leaf_inv.shape[0], leaf_inv.shape[1]
    top_count, dates = top_inv.shape[0], obs_data.shape[0]
    top_each = top_count // groups
    coef_rows = obs_coef.shape[0]
    piece = capacity * coef_rows // LANES
    payload = piece + dates // 2 + 8
    pair = groups // 2
    cuts = 2 if dates % 16 == 0 else 1
    half = dates // cuts
    dma = pltpu.SemaphoreType.DMA
    vmem = pl.BlockSpec(memory_space=pltpu.VMEM)
    hbm = pl.BlockSpec(memory_space=pltpu.HBM)
    results = (
        jax.ShapeDtypeStruct((local, dates, width), F32),
        jax.ShapeDtypeStruct((top_count, dates, width), F32),
    )
    solved = pl.pallas_call(
        functools.partial(kernel, groups, shards, capacity),
        out_shape=results,
        in_specs=[hbm] * 9,
        out_specs=(vmem, vmem),
        scratch_shapes=[
            pltpu.VMEM((1, rows), jnp.int32),
            pltpu.VMEM(obs_coef.shape, F32),
            pltpu.VMEM(obs_data.shape, F32),
            pltpu.SMEM(leaf_map.shape, jnp.int32),
            pltpu.SMEM(leaf_parent.shape, jnp.int32),
            pltpu.VMEM(leaf_inv.shape, F32),
            pltpu.VMEM(leaf_off.shape, F32),
            pltpu.VMEM((top_each, width, width), F32),
            pltpu.VMEM((top_each, dates, width), F32),
            pltpu.VMEM((groups, payload, LANES), F32),
            pltpu.VMEM((groups, payload, LANES), F32),
            pltpu.VMEM((shards, groups, piece, LANES), F32),
            pltpu.VMEM((2, local, width, width), BF16),
            pltpu.VMEM((local, dates, width), F32),
            pltpu.VMEM((cuts, top_count, half, width), F32),
            pltpu.VMEM((cuts, groups // 2, top_each, half, width), F32),
            pltpu.VMEM((cuts, groups // 2, top_each, half, width), F32),
            pltpu.VMEM((cuts, groups // 2, top_each, half, width), F32),
            dma((groups,)),
            dma((groups,)),
            dma((shards, pair)),
            dma((shards, pair)),
            dma((cuts, groups // 2)),
            dma((cuts, groups // 2)),
            dma((cuts, groups // 2)),
            dma((cuts, groups // 2)),
            dma((cuts, groups)),
            dma((cuts, groups)),
            dma((9,)),
        ],
        compiler_params=pltpu.CompilerParams(
            collective_id=0, has_side_effects=True, vmem_limit_bytes=24 * 2**20
        ),
    )(
        *(
            pltpu.with_memory_space_constraint(x, pltpu.HBM)
            for x in (
                obs_target.reshape(1, rows), obs_coef, obs_data, leaf_map, leaf_parent,
                leaf_inv, leaf_off, top_inv, top_rhs,
            )
        )
    )
    return pl.pallas_call(
        write_out,
        out_shape=results,
        in_specs=[vmem, vmem],
        out_specs=(hbm, hbm),
        scratch_shapes=[dma((2,))],
        compiler_params=pltpu.CompilerParams(vmem_limit_bytes=4 * 2**20),
    )(*solved)


def plain(
    obs_coef, obs_data, obs_target, leaf_map, leaf_parent, leaf_inv, leaf_off, top_inv, top_rhs
):
    highest = lax.Precision.HIGHEST
    groups = lax.axis_size("leaf")
    device_index = lax.axis_index("leaf")
    local_count = leaf_inv.shape[0]
    block_width = leaf_inv.shape[1]
    top_count = top_inv.shape[0]
    date_cols = obs_data.shape[0]
    rows_here = obs_target.shape[0]
    leaf_total = leaf_map.shape[0]
    capacity = max(2, 2 * rows_here // groups)
    slots_total = groups * capacity
    all_ids = jnp.arange(leaf_total, dtype=jnp.int32)
    id_match = obs_target[:, None] == all_ids[None, :]
    position = jnp.sum(jnp.where(id_match, leaf_map[None, :], 0), axis=1)
    owner_dev = position // local_count
    member = position % local_count
    row_ids = jnp.arange(rows_here, dtype=jnp.int32)
    earlier = (owner_dev[:, None] == owner_dev[None, :]) & (row_ids[:, None] > row_ids[None, :])
    queue_rank = jnp.sum(earlier.astype(jnp.int32), axis=1)
    target_slot = owner_dev * capacity + queue_rank
    slot_mark = (member + 1).astype(jnp.float32)[None, :]
    fields = jnp.concatenate([obs_coef, obs_data, slot_mark], axis=0)
    placed = jnp.zeros((fields.shape[0], slots_total), F32).at[:, target_slot].set(fields)
    received = lax.all_to_all(placed, "leaf", split_axis=1, concat_axis=1, tiled=True)
    part_coef = received[: obs_coef.shape[0]]
    recv_data = received[obs_coef.shape[0] : -1]
    recv_mark = received[-1:]
    recv_coef = lax.all_gather(part_coef, "rhs", axis=0, tiled=True)
    slot_values = (jnp.arange(local_count, dtype=jnp.int32) + 1).astype(jnp.float32)
    chosen = (recv_mark[0][None, :] == slot_values[:, None]).astype(jnp.float32)
    spread = (recv_data[None, :, :] * chosen[:, None, :]).reshape(
        local_count * date_cols, slots_total
    )
    leaf_rhs = lax.dot_general(
        spread, recv_coef, (((1,), (1,)), ((), ())), precision=highest
    ).reshape(local_count, date_cols, block_width)
    solved = jnp.einsum("ltc,ldc->ltd", leaf_rhs, leaf_inv, precision=highest)
    update = jnp.einsum("ltd,lcd->ltc", solved, leaf_off, precision=highest)
    positions_here = device_index * local_count + jnp.arange(local_count, dtype=jnp.int32)
    holder_match = leaf_map[None, :] == positions_here[:, None]
    parent_here = jnp.sum(jnp.where(holder_match, leaf_parent[None, :], 0), axis=1)
    to_top = (parent_here[:, None] == jnp.arange(top_count, dtype=jnp.int32)[None, :]).astype(
        jnp.float32
    )
    contrib = jnp.einsum("lp,ltc->ptc", to_top, update, precision=highest)
    flat_terms = contrib.reshape(top_count * date_cols, block_width)
    top_total = lax.psum(flat_terms, "leaf").reshape(top_count, date_cols, block_width)
    residue = top_rhs - top_total
    top_solved = jnp.einsum("ptc,pdc->ptd", residue, top_inv, precision=highest)
    top_solution = jnp.einsum("ptd,pdc->ptc", top_solved, top_inv, precision=highest)
    from_top = jnp.einsum("lp,ptc->ltc", to_top, top_solution, precision=highest)
    lifted = jnp.einsum("ltc,lcd->ltd", from_top, leaf_off, precision=highest)
    leaf_solution = jnp.einsum("ltc,lcd->ltd", solved - lifted, leaf_inv, precision=highest)
    return (leaf_solution, top_solution)


def body(*args):
    obs_coef, obs_data, obs_target = args[:3]
    groups = lax.axis_size("leaf")
    coef_rows, rows = obs_coef.shape
    dates = obs_data.shape[0]
    fits = (
        args[7].shape[0] % groups == 0
        and groups % 4 == 0
        and groups & (groups - 1) == 0
        and rows % LANES == 0
        and (2 * rows) % groups == 0
        and LANES % coef_rows == 0
        and (2 * rows // groups) % (8 * (LANES // coef_rows)) == 0
        and coef_rows % 8 == 0
        and dates % 16 == 0
        and 2 * (2 * rows // groups) == LANES
        and args[5].shape[1] == LANES
    )
    return fused(*args) if fits else plain(*args)


def solution(mesh):
    return jax.shard_map(
        body,
        mesh=mesh,
        in_specs=(
            P("rhs", "leaf"),
            P("rhs", "leaf"),
            P("leaf"),
            P(),
            P(),
            P("leaf", None, None),
            P("leaf", None, None),
            P(),
            P(None, "rhs", None),
        ),
        out_specs=(P("leaf", "rhs", None), P(None, "rhs", None)),
        check_vma=False,
    )
```

profile of v0, /device:TPU:0, one launch (start us, length us, event | category | flops | bytes accessed | tf_op | source)
XLA Modules:
  0.0 35.6 jit_solution(7664760876370981101)
XLA Ops:
  0.6 34.1 %shard_map.104 = (f32[4,80,128]{2,1,0:T(8,128)S(1)}, f32[8,80,128]{2,1,0:T(8,128)S(1)}) custom-call(s32[1,256]{1,0:T(1,128)} %bitcast.1, f32[32,256]{1,0:T(8,128)} %coef_h.1, f32[80,256]{1,0:T(8,128)} %data_h.1, s32[32]{0:T(128)} %lmap_h.1, s32[32]{0:T(128)} %lpar_h.1, f32[4,128,128]{2,1,0:T(8,128)} %inv_h.1, f32[4,128,128]{2,1,0:T(8,128)} %off_h.1, ...), custom_call_target="tpu_custom_call" | custom-call | tf_op jit(solution)/shard_map/pallas_call | solution.py:372
  34.8 0.8 %shard_map.105 = (f32[4,80,128]{2,1,0:T(8,128)}, f32[8,80,128]{2,1,0:T(8,128)}) custom-call(f32[4,80,128]{2,1,0:T(8,128)S(1)} %get-tuple-element.4.leaf_v, f32[8,80,128]{2,1,0:T(8,128)S(1)} %get-tuple-element.5.top_v), custom_call_target="tpu_custom_call" | custom-call | tf_op jit(solution)/shard_map/pallas_call | solution.py:420
where the time goes:
time: 35.7 us; the launch traced here: 35.6 us
  Pallas kernels  34.9 us (98%)
  between operations  0.64 us (2%)
    pallas_call x1, Pallas kernels, fused(): pl.pallas_call(functools.partial(kernel, groups, shards, capacity), out_s...  34.1 us
    pallas_call x1, Pallas kernels, fused(): pl.pallas_call(write_out, out_shape=results, in_specs=[vmem, vmem], out_s...  0.8 us

commit v1 on v0

--- a/solution.py
+++ b/solution.py
@@ -359,8 +359,8 @@
     coef_rows = obs_coef.shape[0]
     piece = capacity * coef_rows // LANES
     payload = piece + dates // 2 + 8
-    pair = groups // 2
-    cuts = 2 if dates % 16 == 0 else 1
+    pair = 2
+    cuts = 1
     half = dates // cuts
     dma = pltpu.SemaphoreType.DMA
     vmem = pl.BlockSpec(memory_space=pltpu.VMEM)

time: 35.7 us -> 36.2 us (1.014)
  Pallas kernels: 34.9 us -> 35.4 us
    pallas_call x1, Pallas kernels: 34.1 us -> 34.6 us  [fused(): pl.pallas_call(functools.partial(kernel, groups, shards, capacity), out_s...]
where the time goes in v1:
time: 36.2 us; the launch traced here: 36 us
  Pallas kernels  35.4 us (98%)
  between operations  0.64 us (2%)
    pallas_call x1, Pallas kernels, fused(): pl.pallas_call(functools.partial(kernel, groups, shards, capacity), out_s...  34.6 us
    pallas_call x1, Pallas kernels, fused(): pl.pallas_call(write_out, out_shape=results, in_specs=[vmem, vmem], out_s...  0.8 us

profile of v1, /device:TPU:0, one launch (start us, length us, event | category | flops | bytes accessed | tf_op | source)
XLA Modules:
  0.0 36.0 jit_solution(16447355712377360100)
XLA Ops:
  0.6 34.6 %shard_map.104 = (f32[4,80,128]{2,1,0:T(8,128)S(1)}, f32[8,80,128]{2,1,0:T(8,128)S(1)}) custom-call(s32[1,256]{1,0:T(1,128)} %bitcast.1, f32[32,256]{1,0:T(8,128)} %coef_h.1, f32[80,256]{1,0:T(8,128)} %data_h.1, s32[32]{0:T(128)} %lmap_h.1, s32[32]{0:T(128)} %lpar_h.1, f32[4,128,128]{2,1,0:T(8,128)} %inv_h.1, f32[4,128,128]{2,1,0:T(8,128)} %off_h.1, ...), custom_call_target="tpu_custom_call" | custom-call | tf_op jit(solution)/shard_map/pallas_call | solution.py:372
  35.2 0.8 %shard_map.105 = (f32[4,80,128]{2,1,0:T(8,128)}, f32[8,80,128]{2,1,0:T(8,128)}) custom-call(f32[4,80,128]{2,1,0:T(8,128)S(1)} %get-tuple-element.4.leaf_v, f32[8,80,128]{2,1,0:T(8,128)S(1)} %get-tuple-element.5.top_v), custom_call_target="tpu_custom_call" | custom-call | tf_op jit(solution)/shard_map/pallas_call | solution.py:420
